TPU v7x, 32 devices: a whole 2x2x4 slice. The times are simulated.
32 devices in a mesh: row: 8 (over z, x), reach: 4 (over y, core).
Axes of the slice: x: 2, y: 2, z: 4, core: 2. Of those that a mesh axis runs over, the one named last changes fastest.
Arguments:
- basis: bfloat16 [65536, 128], P(('row', 'reach')), may hold values from -6 to 6
- near_cols: int32 [1024, 7], P(('row', 'reach')), may hold values from 0 to 127, as said below
- near_count: int32 [1024], P(('row', 'reach')), may hold values from 1 to 7
- near_blocks: bfloat16 [1024, 7, 4096], P(('row', 'reach')), may hold values from -0.25 to 0.25
- marker_rows: int32 [512], P(('row', 'reach')), may hold values from 0 to 31
- marker_groups: int32 [512], P(('row', 'reach')), may hold values from 0 to 63, as said below
- marker_count: int32 [32], P(('row', 'reach')), may hold values from 2 to 16
- marker_weights: bfloat16 [512, 4096], P(('row', 'reach')), may hold values from -0.75 to 0.75
- stiffness: float32 [4096], replicated, may hold values from 0.5 to 4
Outputs:
- qfactor: float32 [65536, 128], P(('row', 'reach'))
- rfactor: float32 [128, 128], replicated
Inputs may be any that keep to these rules, and one draw needn't show every extreme that they name: `near_cols`: the first stored block of each block row is the block row itself. `marker_groups`: slot 0 of slab s names group ((64 * s) // 32 + 64 // 2) % 64; slot 1 names (64 * s) // 32; every other slot names that group or the one after it, never beyond 64 - 1.
All inputs are finite; a program needn't handle non-finite values.
Results may differ from a plain program's by a relative error of at most 0.0025.
Values may be sent and summed in bfloat16 or wider, within the bound.
A program may use at most 64 MiB of HBM per device.

v0:
```python
import jax
import jax.numpy as jnp
from jax import lax
from jax.sharding import PartitionSpec as P

BS = 64
NG = 64


def force_of(sums, stiffness):
    scale = lax.rsqrt(1.0 + jnp.mean(sums * sums, axis=1, keepdims=True))
    return (stiffness[:, None] * sums * scale).astype(jnp.bfloat16)


def local(
    basis,
    near_cols,
    near_count,
    near_blocks,
    marker_rows,
    marker_groups,
    marker_count,
    marker_weights,
    stiffness,
):
    slab, stored = near_cols.shape
    width = basis.shape[1]
    side = BS
    slots = marker_rows.shape[0]
    groups = NG
    markers = groups * side
    hp = lax.Precision.HIGHEST
    own = basis.reshape(slab, side, width)
    weights = marker_weights.reshape(slots, side, side)
    mlive = jnp.arange(slots, dtype=jnp.int32) < marker_count[0]
    picked = own[marker_rows]
    partial_value = jnp.einsum("mcj,mcd->mjd", weights, picked, preferred_element_type=jnp.float32)
    partial_flat = partial_value.reshape(slots, side * width)
    onehot = (marker_groups[None, :] == jnp.arange(groups, dtype=jnp.int32)[:, None]) & mlive[
        None, :
    ]
    local_sums = jnp.dot(onehot.astype(jnp.float32), partial_flat, precision=hp).reshape(
        markers, width
    )
    totals = lax.psum(local_sums, ("row", "reach"))
    force = force_of(totals, stiffness)
    force_rows = jnp.dot(
        onehot.T.astype(jnp.bfloat16),
        force.reshape(groups, side * width),
        preferred_element_type=jnp.float32,
    )
    group_basis = lax.all_gather(basis, "reach", axis=0, tiled=True).reshape(-1, side, width)
    live = jnp.arange(stored, dtype=jnp.int32)[None, :] < near_count[:, None]
    fetched = jnp.where(live[:, :, None, None], group_basis[near_cols], jnp.zeros((), jnp.bfloat16))
    blocks = near_blocks.reshape(slab, stored, side, side)
    near = jnp.einsum("bkrc,bkcd->brd", blocks, fetched, preferred_element_type=jnp.float32)
    force_rows = force_rows.astype(jnp.bfloat16).reshape(slots, side, width)
    contrib = jnp.einsum("mcj,mjd->mcd", weights, force_rows, preferred_element_type=jnp.float32)
    rowhot = (
        (marker_rows[None, :] == jnp.arange(slab, dtype=jnp.int32)[:, None]) & mlive[None, :]
    ).astype(jnp.float32)
    spread = jnp.dot(rowhot, contrib.reshape(slots, side * width), precision=hp).reshape(
        slab, side, width
    )
    image = (near + spread).reshape(slab * side, width)
    gram = lax.psum(jnp.dot(image.T, image, precision=hp), ("row", "reach"))
    lower = jnp.linalg.cholesky(gram)
    solved = jax.scipy.linalg.solve_triangular(lower, image.T, lower=True)
    total_rows = slab * side * lax.axis_size(("row", "reach"))
    root = jnp.sqrt(jnp.float32(total_rows))
    return (solved.T * root, lower.T / root)


def solution(mesh):
    return jax.shard_map(
        local,
        mesh=mesh,
        in_specs=(
            P(("row", "reach"), None),
            P(("row", "reach"), None),
            P(("row", "reach")),
            P(("row", "reach"), None, None),
            P(("row", "reach")),
            P(("row", "reach")),
            P(("row", "reach")),
            P(("row", "reach"), None),
            P(),
        ),
        out_specs=(P(("row", "reach"), None), P()),
        check_vma=False,
    )
```

profile of v0, /device:TPU:1, one launch (start us, length us, event | category | flops | bytes accessed | tf_op | source)
XLA Modules:
  0.0 331.3 jit_solution(2423852829834290028)
XLA Ops:
  8.7 0.7 compare_select_fusion.1
  9.4 1.2 reshape.85
  10.5 1.6 gather_fusion.1
  12.5 1.9 fusion.16
  14.3 1.6 reshape.87
  16.8 0.6 copy-done.1
  17.4 4.9 %reshape.83 = bf16[32,7,64,64]{3,2,0,1:T(8,128)(2,1)} reshape(bf16[32,7,4096]{2,0,1:T(8,128)(2,1)S(1)} %copy-done.1) | data formatting | bytes 3670016 | tf_op jit(solution)/shard_map/reshape | solution.py:55
  22.5 136.2 %all-reduce.3.cloned.1.call-done = f32[4096,128]{1,0:T(8,128)} async-done(((f32[4096,128]{1,0:T(8,128)}), f32[4096,128]{1,0:T(8,128)}) %all-reduce.3.cloned.1.call-update) | async-done | bytes 2097168 | tf_op jit(solution)/shard_map/psum | solution.py:45
  158.7 2.4 multiply_reduce_fusion
  161.1 2.3 multiply_convert_fusion
  163.4 0.7 reshape.88
  164.7 0.9 fusion.19
  165.6 4.5 %gather_fusion = bf16[224,64,128]{2,1,0:T(8,128)(2,1)} fusion(bf16[128,64,128]{2,1,0:T(8,128)(2,1)} %bitcast.62, s32[1024]{0:T(1024)S(1)} %pad_clamp_fusion.1), kind=kCustom, calls=%fused_computation | custom fusion | bytes 7340928 | tf_op jit(solution)/shard_map/gather | solution.py:54
  170.1 4.6 %fusion.10 = f32[32,64,128]{2,1,0:T(8,128)S(1)} fusion(bf16[32,7,64,128]{3,2,1,0:T(8,128)(2,1)} %bitcast.63, pred[32,7]{1,0:T(8,128)(4,1)S(1)} %iota_compare_fusion.3, bf16[32,7,64,64]{3,2,0,1:T(8,128)(2,1)} %reshape.83, f32[32,64,128]{2,0,1:T(8,128)S(1)} %fusion.19), kind=kOutput, calls=%fused_computation.12 | convolution fusion | flops 236978176 | bytes 7602400 | tf_op jit(solution)/shard_map/bkrc,bkcd->brd/dot_general | solution.py:56
  174.7 2.4 convolution_bitcast_fusion
  177.2 119.3 %all-reduce.5.cloned.1.call-done = f32[128,128]{0,1:T(8,128)} async-done(((f32[128,128]{0,1:T(8,128)}), f32[128,128]{0,1:T(8,128)}) %all-reduce.5.cloned.1.call-update) | async-done | bytes 65552 | tf_op jit(solution)/shard_map/psum | solution.py:66
  296.6 0.9 copy.23
  297.5 0.9 fusion.23
  298.4 11.7 %cholesky.16 = f32[128,128]{1,0:T(8,128)S(1)} custom-call(f32[128,128]{1,0:T(8,128)S(1)} %fusion.23), custom_call_target="Cholesky" | custom-call | tf_op jit(solution)/shard_map/jit(cholesky)/cholesky | solution.py:67
  310.1 0.6 compare_reduce_fusion
  310.7 0.7 multiply_bitcast_fusion
  311.4 0.7 copy.24
  312.1 9.8 %custom-call.7 = f32[1,128,128]{1,2,0:T(8,128)S(1)} custom-call(f32[1,128,128]{2,1,0:T(8,128)S(1)} %get-tuple-element.7), custom_call_target="InvertDiagBlocksLowerTriangular" | custom-call | tf_op jit(solution)/shard_map/jit(_solve_triangular)/triangular_solve | solution.py:68
  322.0 1.9 convolution_multiply_fusion
  (33 shorter events, 1.9 us)
Async XLA Ops:
  8.0 150.7 %all-reduce.3.cloned.1.call-start = ((), (), s32[]{:S(2)}) async-start(), calls=%async_computation.1 | async-start | bytes 4194304 | tf_op jit(solution)/shard_map/psum | solution.py:45
  15.9 0.7 copy-start.3
  15.9 1.5 copy-start.1
  16.0 149.6 %all-gather.2.cloned.1.call-start = ((), (), s32[]{:S(2)}) async-start(), calls=%async_computation | async-start | bytes 2621440 | tf_op jit(solution)/shard_map/all_gather | solution.py:52
  16.5 280.0 %all-reduce.5.cloned.1.call-start = ((), (), s32[]{:S(2)}) async-start(), calls=%async_computation.2 | async-start | bytes 131072 | tf_op jit(solution)/shard_map/psum | solution.py:66
  17.4 5.0 %copy-start.6 = (s32[32]{0:T(128)S(1)}, s32[32]{0:T(128)}, u32[]{:S(2)}) copy-start(s32[32]{0:T(128)} %param.11) | copy-start | bytes 388
  22.4 138.7 %copy-start.2 = (f32[4096]{0:T(1024)S(1)}, f32[4096]{0:T(1024)}, u32[]{:S(2)}) copy-start(f32[4096]{0:T(1024)} %param.17) | copy-start | bytes 49156
  158.7 2.4 copy-start
  161.1 3.0 copy-start.4
  163.4 1.3 copy-start.5
Sparse Core Ops, SparseCore 0:
  16.1 142.5 all-reduce.2
  177.3 119.1 all-reduce.4
Sparse Core Ops, SparseCore 1:
  18.0 25.5 all-gather.1
where the time goes:
time: 332 us; the launch traced here: 331 us
  waiting for transfers between devices  256 us (77%)
  other arithmetic  29.1 us (9%)
  local copies, waits for them, and re-layouts  17.1 us (5%)
  between operations  16.3 us (5%)
  matrix products  12.5 us (4%)
    psum x1, waiting for transfers between devices, local(): totals = lax.psum(local_sums, ('row', 'reach'))  136 us
    psum x1, waiting for transfers between devices, local(): gram = lax.psum(jnp.dot(image.T, image, precision=hp), ('row', 'reach'))  119 us
    another operation x3, other arithmetic, local(): lower = jnp.linalg.cholesky(gram)  12.4 us
    another operation x1, other arithmetic, local(): solved = jax.scipy.linalg.solve_triangular(lower, image.T, lower=True)  9.81 us
  transfers between devices with their start and end apart: 3, of which 2 were waited for; matrix products, arithmetic and copies ran while one was open for 4% of the time, Pallas kernels for 0%

commit v1 on v0

--- a/solution.py
+++ b/solution.py
@@ -42,7 +42,9 @@
     local_sums = jnp.dot(onehot.astype(jnp.float32), partial_flat, precision=hp).reshape(
         markers, width
     )
-    totals = lax.psum(local_sums, ("row", "reach"))
+    totals = local_sums
+    for name in ("reach", "row"):
+        totals = lax.psum(totals, name)
     force = force_of(totals, stiffness)
     force_rows = jnp.dot(
         onehot.T.astype(jnp.bfloat16),

time: 332 us -> 364 us (1.096)
  waiting for transfers between devices: 256 us -> 291 us
    all_gather x1, waiting for transfers between devices: 0.03 us -> 17.7 us  [local(): lax.all_gather(basis, 'reach', axis=0, tiled=True).reshape(-1, side, width)]
    psum x1 -> x2, waiting for transfers between devices: 136 us -> 153 us  [local(): totals = lax.psum(totals, name)]
  transfers between devices with their start and end apart: 3 -> 4, of which waited for: 2 -> 4; matrix products, arithmetic and copies ran while one was open for 4% -> 3% of each run, Pallas kernels for 0% -> 0%
where the time goes in v1:
time: 364 us
  waiting for transfers between devices  291 us (80%)
  other arithmetic  29.1 us (8%)
  local copies, waits for them, and re-layouts  16.4 us (5%)
  between operations  14.6 us (4%)
  matrix products  12.5 us (3%)
    psum x2, waiting for transfers between devices, local(): totals = lax.psum(totals, name)  153 us
    psum x1, waiting for transfers between devices, local(): gram = lax.psum(jnp.dot(image.T, image, precision=hp), ('row', 'reach'))  119 us
    all_gather x1, waiting for transfers between devices, local(): lax.all_gather(basis, 'reach', axis=0, tiled=True).reshape(-1, side, width)  17.7 us
    another operation x3, other arithmetic, local(): lower = jnp.linalg.cholesky(gram)  12.4 us
    another operation x1, other arithmetic, local(): solved = jax.scipy.linalg.solve_triangular(lower, image.T, lower=True)  9.81 us
  transfers between devices with their start and end apart: 4, of which 4 were waited for; matrix products, arithmetic and copies ran while one was open for 3% of the time, Pallas kernels for 0%

profile of v1, /device:TPU:1, one launch (start us, length us, event | category | flops | bytes accessed | tf_op | source)
XLA Modules:
  0.0 363.5 jit_solution(11165255453511056376)
XLA Ops:
  8.5 1.2 reshape.85
  9.7 1.6 gather_fusion.1
  11.6 1.8 fusion.16
  13.4 1.5 reshape.87
  15.0 53.5 %all-reduce.4.cloned.1.call-done = f32[4096,128]{1,0:T(8,128)} async-done(((f32[4096,128]{1,0:T(8,128)}), f32[4096,128]{1,0:T(8,128)}) %all-reduce.4.cloned.1.call-update) | async-done | bytes 2097168 | tf_op jit(solution)/shard_map/psum | solution.py:47
  68.6 0.7 all-gather.2.cloned.1.call-update
  69.6 5.0 %reshape.83 = bf16[32,7,64,64]{3,2,0,1:T(8,128)(2,1)} reshape(bf16[32,7,4096]{2,0,1:T(8,128)(2,1)S(1)} %copy-done.1) | data formatting | bytes 3670016 | tf_op jit(solution)/shard_map/reshape | solution.py:57
  74.6 99.8 %all-reduce.6.cloned.1.call-done = f32[4096,128]{1,0:T(8,128)} async-done(((f32[4096,128]{1,0:T(8,128)}), f32[4096,128]{1,0:T(8,128)}) %all-reduce.6.cloned.1.call-update) | async-done | bytes 2097168 | tf_op jit(solution)/shard_map/psum | solution.py:47
  174.4 2.4 multiply_reduce_fusion
  176.8 2.3 multiply_convert_fusion
  179.1 0.7 reshape.88
  180.4 0.9 fusion.19
  181.3 17.7 %all-gather.2.cloned.1.call-done = bf16[8192,128]{1,0:T(8,128)(2,1)} async-done(((bf16[2048,128]{1,0:T(8,128)(2,1)}), bf16[8192,128]{1,0:T(8,128)(2,1)}) %all-gather.2.cloned.1.call-update) | async-done | bytes 2097168 | tf_op jit(solution)/shard_map/all_gather | solution.py:54
  199.0 4.5 %gather_fusion = bf16[224,64,128]{2,1,0:T(8,128)(2,1)} fusion(bf16[128,64,128]{2,1,0:T(8,128)(2,1)} %bitcast.62, s32[1024]{0:T(1024)S(1)} %pad_clamp_fusion.1), kind=kCustom, calls=%fused_computation | custom fusion | bytes 7340928 | tf_op jit(solution)/shard_map/gather | solution.py:56
  203.5 4.6 %fusion.10 = f32[32,64,128]{2,1,0:T(8,128)S(1)} fusion(bf16[32,7,64,128]{3,2,1,0:T(8,128)(2,1)} %bitcast.63, pred[32,7]{1,0:T(8,128)(4,1)S(1)} %iota_compare_fusion.3, bf16[32,7,64,64]{3,2,0,1:T(8,128)(2,1)} %reshape.83, f32[32,64,128]{2,0,1:T(8,128)S(1)} %fusion.19), kind=kOutput, calls=%fused_computation.12 | convolution fusion | flops 236978176 | bytes 7602400 | tf_op jit(solution)/shard_map/bkrc,bkcd->brd/dot_general | solution.py:58
  208.2 2.4 convolution_bitcast_fusion
  210.6 119.0 %all-reduce.8.cloned.1.call-done = f32[128,128]{0,1:T(8,128)} async-done(((f32[128,128]{0,1:T(8,128)}), f32[128,128]{0,1:T(8,128)}) %all-reduce.8.cloned.1.call-update) | async-done | bytes 65552 | tf_op jit(solution)/shard_map/psum | solution.py:68
  329.7 0.9 copy.23
  330.6 0.9 fusion.23
  331.4 11.7 %cholesky.16 = f32[128,128]{1,0:T(8,128)S(1)} custom-call(f32[128,128]{1,0:T(8,128)S(1)} %fusion.23), custom_call_target="Cholesky" | custom-call | tf_op jit(solution)/shard_map/jit(cholesky)/cholesky | solution.py:69
  343.8 0.7 multiply_bitcast_fusion
  344.5 0.7 copy.24
  345.2 9.8 %custom-call.7 = f32[1,128,128]{1,2,0:T(8,128)S(1)} custom-call(f32[1,128,128]{2,1,0:T(8,128)S(1)} %get-tuple-element.7), custom_call_target="InvertDiagBlocksLowerTriangular" | custom-call | tf_op jit(solution)/shard_map/jit(_solve_triangular)/triangular_solve | solution.py:70
  355.0 1.9 convolution_multiply_fusion
  (36 shorter events, 2.7 us)
Async XLA Ops:
  7.2 61.4 %all-reduce.4.cloned.1.call-start = ((), (), s32[]{:S(2)}) async-start(), calls=%async_computation.1 | async-start | bytes 4194304 | tf_op jit(solution)/shard_map/psum | solution.py:47
  15.0 54.4 %copy-start.3 = (s32[32,7]{0,1:T(8,128)S(1)}, s32[32,7]{0,1:T(8,128)}, u32[]{:S(2)}) copy-start(s32[32,7]{0,1:T(8,128)} %param.10) | copy-start | bytes 2692
  15.0 54.6 %copy-start.1 = (bf16[32,7,4096]{2,0,1:T(8,128)(2,1)S(1)}, bf16[32,7,4096]{2,0,1:T(8,128)(2,1)}, u32[]{:S(2)}) copy-start(bf16[32,7,4096]{2,0,1:T(8,128)(2,1)} %param.12) | copy-start | bytes 5505028
  15.0 159.4 %all-reduce.6.cloned.1.call-start = ((), (), s32[]{:S(2)}) async-start(), calls=%async_computation.2 | async-start | bytes 4194304 | tf_op jit(solution)/shard_map/psum | solution.py:47
  68.5 130.5 %all-gather.2.cloned.1.call-start = ((), (), s32[]{:S(2)}) async-start(), calls=%async_computation | async-start | bytes 2621440 | tf_op jit(solution)/shard_map/all_gather | solution.py:54
  69.3 260.4 %all-reduce.8.cloned.1.call-start = ((), (), s32[]{:S(2)}) async-start(), calls=%async_computation.3 | async-start | bytes 131072 | tf_op jit(solution)/shard_map/psum | solution.py:68
  69.6 5.0 %copy-start.6 = (s32[32]{0:T(128)S(1)}, s32[32]{0:T(128)}, u32[]{:S(2)}) copy-start(s32[32]{0:T(128)} %param.11) | copy-start | bytes 388
  74.5 102.2 %copy-start.2 = (f32[4096]{0:T(1024)S(1)}, f32[4096]{0:T(1024)}, u32[]{:S(2)}) copy-start(f32[4096]{0:T(1024)} %param.17) | copy-start | bytes 49156
  174.4 2.4 copy-start
  176.8 3.0 copy-start.4
  179.1 1.3 copy-start.5
Sparse Core Ops, SparseCore 0:
  15.1 53.3 all-reduce.3
  72.6 101.7 all-reduce.5
  176.0 22.9 all-gather.1
  210.7 118.8 all-reduce.7
